TPU v7x, 512 devices: a whole 4x4x16 slice. The times are simulated.
512 devices in a mesh: batch: 16 (over y, x), centre: 32 (over z, core).
Axes of the slice: x: 4, y: 4, z: 16, core: 2. Of those that a mesh axis runs over, the one named last changes fastest.
Arguments:
- pool: float32 [4096, 1024], P('batch', 'centre'), may hold values from -4.5 to 4.5
- sample_index: int32 [2048], P('batch'), may hold values from 0 to 255
- targets: float32 [2048, 256], P('batch'), may hold values from -6 to 6
- centres: float32 [8192, 1024], P(('batch', 'centre')), may hold values from -4.5 to 4.5
- coeffs: float32 [8192, 256], P(('batch', 'centre')), may hold values from -6 to 6
- eigvecs: float32 [8192, 1024], P(('batch', 'centre')), may hold values from -0.1875 to 0.1875
- eigscale: float32 [1024], replicated, may hold values from 0.1 to 0.95
Outputs:
- new_coeffs: float32 [8192, 256], P(('batch', 'centre'))
Inputs may be any that keep to these rules, and one draw needn't show every extreme that they name: `sample_index`: each batch row's sample lies in the block of 256 training samples held by its own batch group; the index counts within that block.
All inputs are finite; a program needn't handle non-finite values.
Results may differ from a plain program's by a relative error of at most 0.0003.
Values sent between devices are 32-bit elements; how exact they have to be, the bound alone decides.
No kernel may reach another device: no remote copies, remote signals or barrier semaphores. Data moves between devices by JAX's collectives and lax.ppermute only.
A program may use at most 64 MiB of HBM per device.

v0:
```python
import jax
import jax.numpy as jnp
from jax import lax
from jax.sharding import Mesh
from jax.sharding import PartitionSpec as P

PLANE = "plane"
ORDER = [[2, 12, 0, 14, 1, 5, 3, 7, 10, 4, 8, 6, 9, 13, 11, 15]]
FAR = "z_far"
NEAR = "z_near"
CORE = "core"
NEAR_CORE = ("z_near", "core")
CENTRE = ("z_far", "z_near", "core")
NEAR_ORDER = [[0, 1, 3, 2]]
NEAR_CORE_ORDER = [[2 * near + core for near in NEAR_ORDER[0] for core in range(2)]]
EVERY = ("plane", "z_far", "z_near", "core")


def product(left, right, left_dim, right_dim, precision=lax.Precision.HIGH):
    return lax.dot_general(
        left,
        right,
        (((left_dim,), (right_dim,)), ((), ())),
        precision=precision,
        preferred_element_type=jnp.float32,
    )


def swapped(value):
    return lax.ppermute(value, CORE, [(0, 1), (1, 0)])


def exchanged(blocks, axis, groups=None):
    return lax.all_to_all(
        blocks, axis, split_axis=0, concat_axis=0, axis_index_groups=groups, tiled=True
    )


def to_all(value, axis, groups=None):
    return exchanged(jnp.broadcast_to(value, (lax.axis_size(axis), *value.shape)), axis, groups)


def on_device(pool, sample_index, targets, centres, coeffs, eigvecs, eigscale):
    n_plane = lax.axis_size(PLANE)
    n_near = lax.axis_size(NEAR)
    n_core = lax.axis_size(CORE)
    own, width = centres.shape
    rows = sample_index.shape[0]
    outs = coeffs.shape[1]
    total_centres = own * n_plane * lax.axis_size(CENTRE)
    total_rows = rows * n_plane
    core = lax.axis_index(CORE)
    merged = jnp.concatenate([centres, coeffs, eigvecs], axis=1)
    group = to_all(merged, PLANE, ORDER).reshape(own * n_plane, -1)
    chosen = lax.broadcasted_iota(jnp.int32, (pool.shape[0], rows), 0) == sample_index[None, :]
    picked = product(pool, chosen.astype(jnp.float32), 0, 0, lax.Precision.HIGHEST)
    batch_t = lax.all_gather(picked, CENTRE, axis=0, tiled=True)
    group, batch_t = lax.optimization_barrier((group, batch_t))
    zrows, terms = (group[:, :width], group[:, width:])
    kernel = jnp.exp(product(batch_t, zrows, 0, 1) * (1.0 / jnp.sqrt(jnp.float32(width))))
    tall = rows // (n_near * n_core)
    by_core = kernel.reshape(n_near, n_core, tall, -1)

    def term_sums(by_core, of_core):
        taken = lax.dynamic_index_in_dim(by_core, of_core, 1, keepdims=False)
        return product(taken.reshape(rows // n_core, -1), terms, 1, 0)

    give, kept_rows = lax.optimization_barrier((term_sums(by_core, 1 - core), by_core))
    come, keep = lax.optimization_barrier((swapped(give), term_sums(kept_rows, core)))
    part = come + keep
    near_sum = exchanged(part.reshape(n_near, tall, -1), NEAR, NEAR_ORDER).sum(axis=0)
    own_sum = lax.all_gather(near_sum, FAR, axis=0).sum(axis=0)
    whole = lax.all_gather(
        own_sum, NEAR_CORE, axis_index_groups=NEAR_CORE_ORDER, axis=0, tiled=True
    )
    model_norm = 1.0 / jnp.sqrt(jnp.float32(total_centres))
    residual = whole[:, :outs] * model_norm - targets
    scaled = whole[:, outs:] * eigscale
    weight = kernel - product(scaled, terms[:, outs:], 1, 1)
    change = product(weight, residual, 0, 0)
    change = exchanged(change.reshape(n_plane, own, outs), PLANE, ORDER).sum(axis=0)
    step_size = 0.5 * jnp.sqrt(jnp.float32(total_centres) / jnp.float32(total_rows))
    return coeffs - step_size * model_norm * change


def solution(mesh):
    finer = Mesh(mesh.devices.reshape(16, 4, 4, 2), EVERY)
    placed = (
        P(PLANE, CENTRE),
        P(PLANE),
        P(PLANE, None),
        P(EVERY, None),
        P(EVERY, None),
        P(EVERY, None),
        P(),
    )
    return jax.shard_map(
        on_device, mesh=finer, in_specs=placed, out_specs=P(EVERY, None), check_vma=False
    )
```

profile of v0, /device:TPU:1, one launch (start us, length us, event | category | flops | bytes accessed | tf_op | source)
XLA Modules:
  0.0 117.7 jit_solution(12965106669751825569)
XLA Ops:
  0.0 0.0 copy-start
  0.0 0.9 pad_maximum_fusion
  0.9 1.6 %broadcast_in_dim.2 = f32[16,16,2304]{2,1,0:T(8,128)} broadcast(f32[16,2304]{1,0:T(8,128)S(1)} %pad_maximum_fusion), dimensions={1,2} | broadcast | bytes 2506752 | tf_op jit(solution)/shard_map/broadcast_in_dim | solution.py:40
  2.6 8.5 %all-to-all-start = ((f32[16,16,2304]{2,1,0:T(8,128)}), f32[16,16,2304]{2,1,0:T(8,128)S(1)}, u32[]{:S(2)}, u32[]{:S(2)}) async-start(f32[16,16,2304]{2,1,0:T(8,128)} %broadcast_in_dim.2), calls=%async_computation | async-start | bytes 4718592 | tf_op jit(solution)/shard_map/all_to_all | solution.py:34
  11.1 0.0 copy-done
  11.1 0.2 convolution_bitcast_fusion
  11.3 38.7 %all_gather.12 = f32[1024,128]{1,0:T(8,128)S(1)} all-gather(f32[32,128]{1,0:T(8,128)S(1)} %convolution_bitcast_fusion), channel_id=1, replica_groups=mesh['plane'=16,'z_far'=4,'z_near'=4,'core'=2] {'z_far','z_near','core'}, dimensions={0}, use_global_device_ids=true | all-gather | bytes 540672 | tf_op jit(solution)/shard_map/all_gather | solution.py:57
  50.0 0.0 all-to-all-done
  50.0 0.6 fusion.4
  50.6 0.5 fusion.2
  51.1 2.1 %collective-permute-start = (f32[64,1280]{1,0:T(8,128)S(1)}, f32[64,1280]{1,0:T(8,128)S(1)}, u32[]{:S(2)}, u32[]{:S(2)}) collective-permute-start(f32[64,1280]{1,0:T(8,128)S(1)} %fusion.2), channel_id=1, source_target_pairs={{0,1},{1,0},{2,3},{3,2},{4,5},{5,4},{6,7},{7,6},{8,9},{9,8},{10,11... | collective-permute-start | bytes 983048 | tf_op jit(solution)/shard_map/ppermute | solution.py:30
  53.2 0.0 copy-start.3
  53.3 0.5 fusion
  53.8 0.9 collective-permute-done
  54.7 0.0 copy-start.1
  54.7 12.1 %all_to_all.15 = f32[4,16,1280]{2,1,0:T(8,128)S(1)} all-to-all(f32[4,16,1280]{2,1,0:T(8,128)S(1)} %bitcast.19), channel_id=1, replica_groups={{0,2,6,4},{1,3,7,5},{8,10,14,12},{9,11,15,13},{16,18,22,20},{17,19,23,2..., dimensions={0} | all-to-all | bytes 655360 | tf_op jit(solution)/shard_map/all_to_all | solution.py:34
  66.8 0.0 copy-start.2
  66.8 17.7 %all-gather = f32[64,1280]{1,0:T(8,128)S(1)} all-gather(f32[16,1280]{1,0:T(8,128)S(1)} %reduce_sum.27), channel_id=2, replica_groups=mesh['plane'=16,'z_far'=4,'z_near'=4,'core'=2] {'z_far'}, dimensions={0}, use_global_device_ids=true | all-gather | bytes 409600 | tf_op jit(solution)/shard_map/all_gather | solution.py:72
  84.5 17.0 %all_gather.15 = f32[128,1280]{1,0:T(8,128)S(1)} all-gather(f32[16,1280]{1,0:T(8,128)S(1)} %reduce_sum.28), channel_id=1, replica_groups={{0,1,2,3,6,7,4,5},{8,9,10,11,14,15,12,13},{16,17,18,19,22,23,20,21},{24..., dimensions={0}, use_global_device_ids=true | all-gather | bytes 737280 | tf_op jit(solution)/shard_map/all_gather | solution.py:73
  101.5 0.7 convolution_subtract_fusion
  102.1 0.3 fusion.9
  102.4 14.6 %all_to_all.16 = f32[16,16,256]{2,1,0:T(8,128)S(1)} all-to-all(f32[16,16,256]{2,1,0:T(8,128)S(1)} %bitcast.22), channel_id=1, replica_groups={{64,384,0,448,32,160,96,224,320,128,256,192,288,416,352,480},{65,385,1,..., dimensions={0} | all-to-all | bytes 524288 | tf_op jit(solution)/shard_map/all_to_all | solution.py:34
  117.1 0.0 copy-done.2
  117.1 0.6 multiply_subtract_fusion
  (10 shorter events, 0.1 us)
Async XLA Ops:
  0.0 11.1 %copy-start = (f32[256,32]{0,1:T(8,128)S(1)}, f32[256,32]{0,1:T(8,128)}, u32[]{:S(2)}) copy-start(f32[256,32]{0,1:T(8,128)} %param.7) | copy-start | bytes 98308
  2.6 8.6 %copy-start.4 = (s32[128]{0:T(128)S(1)}, s32[128]{0:T(128)}, u32[]{:S(2)}) copy-start(s32[128]{0:T(128)} %param.8) | copy-start | bytes 1540
  2.6 47.5 %all-to-all-start = ((f32[16,16,2304]{2,1,0:T(8,128)}), f32[16,16,2304]{2,1,0:T(8,128)S(1)}, u32[]{:S(2)}, u32[]{:S(2)}) async-start(f32[16,16,2304]{2,1,0:T(8,128)} %broadcast_in_dim.2), calls=%async_computation | async-start | bytes 4718592 | tf_op jit(solution)/shard_map/all_to_all | solution.py:34
  51.1 3.5 %collective-permute-start = (f32[64,1280]{1,0:T(8,128)S(1)}, f32[64,1280]{1,0:T(8,128)S(1)}, u32[]{:S(2)}, u32[]{:S(2)}) collective-permute-start(f32[64,1280]{1,0:T(8,128)S(1)} %fusion.2), channel_id=1, source_target_pairs={{0,1},{1,0},{2,3},{3,2},{4,5},{5,4},{6,7},{7,6},{8,9},{9,8},{10,11... | collective-permute-start | bytes 983048 | tf_op jit(solution)/shard_map/ppermute | solution.py:30
  53.2 48.2 %copy-start.3 = (f32[1024]{0:T(1024)S(1)}, f32[1024]{0:T(1024)}, u32[]{:S(2)}) copy-start(f32[1024]{0:T(1024)} %param.13) | copy-start | bytes 12292
  54.7 47.4 %copy-start.1 = (f32[128,256]{1,0:T(8,128)S(1)}, f32[128,256]{1,0:T(8,128)}, u32[]{:S(2)}) copy-start(f32[128,256]{1,0:T(8,128)} %param.9) | copy-start | bytes 393220
  66.8 50.3 %copy-start.2 = (f32[16,256]{1,0:T(8,128)S(1)}, f32[16,256]{1,0:T(8,128)}, u32[]{:S(2)}) copy-start(f32[16,256]{1,0:T(8,128)} %param.11) | copy-start | bytes 49156
where the time goes:
time: 118 us
  blocking collectives  100 us (85%)
  starting transfers between devices  10.6 us (9%)
  matrix products  2.72 us (2%)
  local copies, waits for them, and re-layouts  1.7 us (1%)
  other arithmetic  1.61 us (1%)
    all_gather x1, blocking collectives, on_device(): batch_t = lax.all_gather(picked, CENTRE, axis=0, tiled=True)  38.7 us
    all_to_all x2, blocking collectives, exchanged(): lax.all_to_all(blocks, axis, split_axis=0, concat_axis=0, axis_index_grou...  26.7 us
    all_gather x1, blocking collectives, on_device(): own_sum = lax.all_gather(near_sum, FAR, axis=0).sum(axis=0)  17.7 us
    all_gather x1, blocking collectives, on_device(): lax.all_gather(own_sum, NEAR_CORE, axis_index_groups=NEAR_CORE_ORDER, axi...  17 us
    all_to_all x1, starting transfers between devices, exchanged(): lax.all_to_all(blocks, axis, split_axis=0, concat_axis=0, axis_index_grou...  8.54 us
    dot_general x6, matrix products, product(): lax.dot_general(left, right, (((left_dim,), (right_dim,)), ((), ())), pre...  2.72 us
  transfers between devices with their start and end apart: 2, of which 1 were waited for; matrix products, arithmetic and copies ran while one was open for 1% of the time, Pallas kernels for 0%

commit v1 on v0

--- a/solution.py
+++ b/solution.py
@@ -54,7 +54,13 @@
     group = to_all(merged, PLANE, ORDER).reshape(own * n_plane, -1)
     chosen = lax.broadcasted_iota(jnp.int32, (pool.shape[0], rows), 0) == sample_index[None, :]
     picked = product(pool, chosen.astype(jnp.float32), 0, 0, lax.Precision.HIGHEST)
-    batch_t = lax.all_gather(picked, CENTRE, axis=0, tiled=True)
+
+    def series_draft(mine):
+        raw_out = jnp.stack([mine] * lax.psum(1, CENTRE), axis=0)
+        low = lax.all_to_all(raw_out, CENTRE, 0, 0)
+        return jnp.concatenate(low, axis=0)
+
+    batch_t = series_draft(picked)
     group, batch_t = lax.optimization_barrier((group, batch_t))
     zrows, terms = (group[:, :width], group[:, width:])
     kernel = jnp.exp(product(batch_t, zrows, 0, 1) * (1.0 / jnp.sqrt(jnp.float32(width))))

time: 118 us -> 165 us (1.40)
  waiting for transfers between devices: 0.91 us -> 62.9 us
  blocking collectives: 100 us -> 66 us
  starting transfers between devices: 10.6 us -> 27.6 us
    all_gather x1 -> x0, blocking collectives: 38.7 us -> none  [on_device(): batch_t = lax.all_gather(picked, CENTRE, axis=0, tiled=True)]
    all_to_all x0 -> x1, waiting for transfers between devices: none -> 32.6 us  [series_draft(): low = lax.all_to_all(raw_out, CENTRE, 0, 0)]
    all_to_all x1, waiting for transfers between devices: 0.01 us -> 29.6 us  [exchanged(): lax.all_to_all(blocks, axis, split_axis=0, concat_axis=0, axis_index_grou...]
    all_to_all x0 -> x1, starting transfers between devices: none -> 16.7 us  [series_draft(): low = lax.all_to_all(raw_out, CENTRE, 0, 0)]
    all_gather x1, blocking collectives: 17 us -> 20.9 us  [on_device(): lax.all_gather(own_sum, NEAR_CORE, axis_index_groups=NEAR_CORE_ORDER, axi...]
  transfers between devices with their start and end apart: 2 -> 3, of which waited for: 1 -> 3; matrix products, arithmetic and copies ran while one was open for 1% -> 1% of each run, Pallas kernels for 0% -> 0%
where the time goes in v1:
time: 165 us
  blocking collectives  66 us (40%)
  waiting for transfers between devices  62.9 us (38%)
  starting transfers between devices  27.6 us (17%)
  matrix products  3.37 us (2%)
  local copies, waits for them, and re-layouts  3.3 us (2%)
    all_to_all x1, waiting for transfers between devices, series_draft(): low = lax.all_to_all(raw_out, CENTRE, 0, 0)  32.6 us
    all_to_all x1, waiting for transfers between devices, exchanged(): lax.all_to_all(blocks, axis, split_axis=0, concat_axis=0, axis_index_grou...  29.6 us
    all_to_all x2, blocking collectives, exchanged(): lax.all_to_all(blocks, axis, split_axis=0, concat_axis=0, axis_index_grou...  27.2 us
    all_gather x1, blocking collectives, on_device(): lax.all_gather(own_sum, NEAR_CORE, axis_index_groups=NEAR_CORE_ORDER, axi...  20.9 us
    all_gather x1, blocking collectives, on_device(): own_sum = lax.all_gather(near_sum, FAR, axis=0).sum(axis=0)  18 us
    all_to_all x1, starting transfers between devices, series_draft(): low = lax.all_to_all(raw_out, CENTRE, 0, 0)  16.7 us
    all_to_all x1, starting transfers between devices, exchanged(): lax.all_to_all(blocks, axis, split_axis=0, concat_axis=0, axis_index_grou...  7.58 us
    dot_general x6, matrix products, product(): lax.dot_general(left, right, (((left_dim,), (right_dim,)), ((), ())), pre...  3.37 us
  transfers between devices with their start and end apart: 3, of which 3 were waited for; matrix products, arithmetic and copies ran while one was open for 1% of the time, Pallas kernels for 0%

profile of v1, /device:TPU:1, one launch (start us, length us, event | category | flops | bytes accessed | tf_op | source)
XLA Modules:
  0.0 164.9 jit_solution(1047168423429885675)
XLA Ops:
  0.0 0.8 copy-done
  0.8 0.8 convolution_bitcast_fusion
  1.6 0.9 stack.2
  2.4 16.7 %all-to-all-start.1 = ((f32[32,32,128]{2,1,0:T(8,128)}), f32[32,32,128]{2,1,0:T(8,128)S(1)}, u32[]{:S(2)}, u32[]{:S(2)}) async-start(f32[32,32,128]{2,1,0:T(8,128)} %stack.2), calls=%async_computation.1 | async-start | bytes 1048576 | tf_op jit(solution)/shard_map/all_to_all | solution.py:60
  19.2 0.9 pad_maximum_fusion
  20.1 32.6 %all-to-all-done.1 = f32[32,32,128]{2,1,0:T(8,128)S(1)} async-done(((f32[32,32,128]{2,1,0:T(8,128)}), f32[32,32,128]{2,1,0:T(8,128)S(1)}, u32[]{:S(2)}, u32[]{:S(2)}) %all-to-all-start.1) | async-done | bytes 524320 | tf_op jit(solution)/shard_map/all_to_all | solution.py:60
  52.7 1.6 broadcast_in_dim.2
  54.3 7.6 %all-to-all-start = ((f32[16,16,2304]{2,1,0:T(8,128)}), f32[16,16,2304]{2,1,0:T(8,128)S(1)}, u32[]{:S(2)}, u32[]{:S(2)}) async-start(f32[16,16,2304]{2,1,0:T(8,128)} %broadcast_in_dim.2), calls=%async_computation | async-start | bytes 4718592 | tf_op jit(solution)/shard_map/all_to_all | solution.py:34
  61.9 29.6 %all-to-all-done = f32[16,16,2304]{2,1,0:T(8,128)S(1)} async-done(((f32[16,16,2304]{2,1,0:T(8,128)}), f32[16,16,2304]{2,1,0:T(8,128)S(1)}, u32[]{:S(2)}, u32[]{:S(2)}) %all-to-all-start) | async-done | bytes 2359328 | tf_op jit(solution)/shard_map/all_to_all | solution.py:34
  91.6 0.6 fusion.4
  92.2 0.5 fusion.2
  92.7 3.2 %collective-permute-start = (f32[64,1280]{1,0:T(8,128)S(1)}, f32[64,1280]{1,0:T(8,128)S(1)}, u32[]{:S(2)}, u32[]{:S(2)}) collective-permute-start(f32[64,1280]{1,0:T(8,128)S(1)} %fusion.2), channel_id=1, source_target_pairs={{0,1},{1,0},{2,3},{3,2},{4,5},{5,4},{6,7},{7,6},{8,9},{9,8},{10,11... | collective-permute-start | bytes 983048 | tf_op jit(solution)/shard_map/ppermute | solution.py:30
  96.0 0.0 copy-start.3
  96.0 0.5 fusion
  96.5 0.7 collective-permute-done
  97.2 0.0 copy-start.1
  97.2 15.4 %all_to_all.20 = f32[4,16,1280]{2,1,0:T(8,128)S(1)} all-to-all(f32[4,16,1280]{2,1,0:T(8,128)S(1)} %bitcast.21), channel_id=1, replica_groups={{0,2,6,4},{1,3,7,5},{8,10,14,12},{9,11,15,13},{16,18,22,20},{17,19,23,2..., dimensions={0} | all-to-all | bytes 655360 | tf_op jit(solution)/shard_map/all_to_all | solution.py:34
  112.6 0.0 copy-start.2
  112.6 18.0 %all-gather = f32[64,1280]{1,0:T(8,128)S(1)} all-gather(f32[16,1280]{1,0:T(8,128)S(1)} %reduce_sum.27), channel_id=2, replica_groups=mesh['plane'=16,'z_far'=4,'z_near'=4,'core'=2] {'z_far'}, dimensions={0}, use_global_device_ids=true | all-gather | bytes 409600 | tf_op jit(solution)/shard_map/all_gather | solution.py:78
  130.6 20.9 %all_gather.11 = f32[128,1280]{1,0:T(8,128)S(1)} all-gather(f32[16,1280]{1,0:T(8,128)S(1)} %reduce_sum.28), channel_id=1, replica_groups={{0,1,2,3,6,7,4,5},{8,9,10,11,14,15,12,13},{16,17,18,19,22,23,20,21},{24..., dimensions={0}, use_global_device_ids=true | all-gather | bytes 737280 | tf_op jit(solution)/shard_map/all_gather | solution.py:79
  151.5 0.7 convolution_subtract_fusion
  152.2 0.3 fusion.9
  152.5 11.8 %all_to_all.21 = f32[16,16,256]{2,1,0:T(8,128)S(1)} all-to-all(f32[16,16,256]{2,1,0:T(8,128)S(1)} %bitcast.24), channel_id=1, replica_groups={{64,384,0,448,32,160,96,224,320,128,256,192,288,416,352,480},{65,385,1,..., dimensions={0} | all-to-all | bytes 524288 | tf_op jit(solution)/shard_map/all_to_all | solution.py:34
  164.3 0.6 multiply_subtract_fusion
  (10 shorter events, 0.1 us)
Async XLA Ops:
  0.0 0.8 copy-start
  2.4 50.3 %all-to-all-start.1 = ((f32[32,32,128]{2,1,0:T(8,128)}), f32[32,32,128]{2,1,0:T(8,128)S(1)}, u32[]{:S(2)}, u32[]{:S(2)}) async-start(f32[32,32,128]{2,1,0:T(8,128)} %stack.2), calls=%async_computation.1 | async-start | bytes 1048576 | tf_op jit(solution)/shard_map/all_to_all | solution.py:60
  54.3 37.2 %all-to-all-start = ((f32[16,16,2304]{2,1,0:T(8,128)}), f32[16,16,2304]{2,1,0:T(8,128)S(1)}, u32[]{:S(2)}, u32[]{:S(2)}) async-start(f32[16,16,2304]{2,1,0:T(8,128)} %broadcast_in_dim.2), calls=%async_computation | async-start | bytes 4718592 | tf_op jit(solution)/shard_map/all_to_all | solution.py:34
  92.7 4.5 %collective-permute-start = (f32[64,1280]{1,0:T(8,128)S(1)}, f32[64,1280]{1,0:T(8,128)S(1)}, u32[]{:S(2)}, u32[]{:S(2)}) collective-permute-start(f32[64,1280]{1,0:T(8,128)S(1)} %fusion.2), channel_id=1, source_target_pairs={{0,1},{1,0},{2,3},{3,2},{4,5},{5,4},{6,7},{7,6},{8,9},{9,8},{10,11... | collective-permute-start | bytes 983048 | tf_op jit(solution)/shard_map/ppermute | solution.py:30
  96.0 55.5 %copy-start.3 = (f32[1024]{0:T(1024)S(1)}, f32[1024]{0:T(1024)}, u32[]{:S(2)}) copy-start(f32[1024]{0:T(1024)} %param.13) | copy-start | bytes 12292
  97.2 54.9 %copy-start.1 = (f32[128,256]{1,0:T(8,128)S(1)}, f32[128,256]{1,0:T(8,128)}, u32[]{:S(2)}) copy-start(f32[128,256]{1,0:T(8,128)} %param.9) | copy-start | bytes 393220
  112.6 51.7 %copy-start.2 = (f32[16,256]{1,0:T(8,128)S(1)}, f32[16,256]{1,0:T(8,128)}, u32[]{:S(2)}) copy-start(f32[16,256]{1,0:T(8,128)} %param.11) | copy-start | bytes 49156
